TPU v7x, 256 devices: a whole 4x4x8 slice. The times are simulated.
256 devices in a mesh: example: 64 (over x, z, core), feature: 4 (over y).
Axes of the slice: x: 4, y: 4, z: 8, core: 2. Of those that a mesh axis runs over, the one named last changes fastest.
Arguments:
- embeddings: bfloat16 [36864, 16384], P('example', 'feature'), may hold values from -16 to 16
- subspace: bfloat16 [16384, 128], P('feature'), may hold values from -0.046875 to 0.046875
- noise_levels: int32 [16384, 128], P('feature'), may hold values from -16 to 16
- targets: int32 [2048], replicated, may hold values from 0 to 16383
Outputs:
- embedding_grad: bfloat16 [36864, 16384], P('example', 'feature')
All inputs are finite; a program needn't handle non-finite values.
Results may differ from a plain program's by a relative error of at most 0.0085.
Values may be sent and summed in bfloat16 or wider, within the bound.
A program may use at most 64 MiB of HBM per device.

v0:
```python
import jax
import jax.numpy as jnp
from jax import lax
from jax.sharding import PartitionSpec as P

NOISE_STEP = 1.0 / 4096.0
HIGH = lax.Precision.HIGHEST


def transposed(former, latter, precision=None):
    return lax.dot_general(
        former,
        latter,
        (((0,), (0,)), ((), ())),
        precision=precision,
        preferred_element_type=jnp.float32,
    )


def by_columns(former, latter):
    return lax.dot_general(
        former, latter, (((1,), (1,)), ((), ())), preferred_element_type=jnp.float32
    )


def count_rows(targets, first, length):
    local = targets - first
    inside = (local >= 0) & (local < length)
    slots = jnp.where(inside, local, length)
    ones = jnp.ones(targets.shape, jnp.float32)
    return jax.ops.segment_sum(ones, slots, num_segments=length + 1)[:length]


def upper_factor(gram_matrix):
    return jnp.linalg.cholesky(gram_matrix).T


def factorize(gram_matrix):
    lower_factor = jnp.linalg.cholesky(gram_matrix)
    identity = jnp.eye(gram_matrix.shape[0], dtype=jnp.float32)
    inverse_factor = jax.scipy.linalg.solve_triangular(lower_factor, identity, lower=True)
    gram_inverse = jnp.dot(inverse_factor.T, inverse_factor, precision=HIGH)
    return (inverse_factor, gram_inverse)


def on_device(embeddings, subspace, noise_levels, targets):
    row_count, local_width = embeddings.shape
    examples = lax.axis_size("example")
    total_rows = row_count * examples
    projected = lax.psum(
        jnp.dot(embeddings, subspace, preferred_element_type=jnp.float32), "feature"
    )
    projected_low = projected.astype(jnp.bfloat16)
    feature_first = lax.axis_index("feature") * local_width
    share = local_width // examples
    summed = lax.psum_scatter(
        transposed(embeddings, projected_low), "example", scatter_dimension=0, tiled=True
    )
    offset = lax.axis_index("example") * share
    noise_part = lax.dynamic_slice_in_dim(noise_levels, offset, share, 0)
    image = summed / total_rows + NOISE_STEP * noise_part.astype(jnp.float32)
    row_counts = count_rows(targets, feature_first + offset, share)
    gram_matrix = lax.psum(transposed(image, image, HIGH), ("example", "feature"))
    inverse_factor, gram_inverse = factorize(gram_matrix)
    orthonormal = jnp.dot(image, inverse_factor.T, precision=HIGH)
    alignment = lax.psum(
        transposed(orthonormal * row_counts[:, None], orthonormal, HIGH), ("example", "feature")
    )
    factor_grad = 2.0 * jnp.dot(alignment, inverse_factor, precision=HIGH)
    unused, pull_back = jax.vjp(upper_factor, gram_matrix)
    gram_grad = pull_back(factor_grad)[0]
    image_grad = jnp.dot(image, gram_grad + gram_grad.T, precision=HIGH) - 2.0 * row_counts[
        :, None
    ] * jnp.dot(image, gram_inverse, precision=HIGH)
    grad_low = image_grad.astype(jnp.bfloat16)
    grad_low = lax.all_gather(grad_low, "example", axis=0, tiled=True)
    back_sum = lax.psum(
        jnp.dot(embeddings, grad_low, preferred_element_type=jnp.float32), "feature"
    )
    back_rows = back_sum.astype(jnp.bfloat16)
    result = by_columns(projected_low, grad_low) + by_columns(back_rows, subspace)
    return result.astype(jnp.bfloat16)


def solution(mesh):
    in_specs = (P("example", "feature"), P("feature", None), P("feature", None), P())
    out_specs = P("example", "feature")
    return jax.shard_map(
        on_device, mesh=mesh, in_specs=in_specs, out_specs=out_specs, check_vma=False
    )
```

profile of v0, /device:TPU:2, one launch (start us, length us, event | category | flops | bytes accessed | tf_op | source)
XLA Modules:
  0.0 797.7 jit_solution(3288870860719686440)
XLA Ops:
  6.5 4.2 fusion.45
  10.7 20.2 %all-reduce.8 = bf16[576,128]{1,0:T(8,128)(2,1)S(1)} all-reduce(f32[576,128]{1,0:T(8,128)S(1)} %fusion.45), channel_id=1, replica_groups=mesh['example'=64,'feature'=4] {'feature'}, use_global_device_ids=true, to_apply=%region_0.0 | all-reduce | flops 73728 | bytes 442368 | tf_op jit(solution)/shard_map/psum | solution.py:50
  30.9 4.7 convolution_bitcast_fusion
  35.6 2.9 copy.14
  38.8 14.7 %scatter_custom_fusion = f32[65]{0:T(128)S(1)} fusion(s32[2048]{0:T(1024)S(1)} %and_select_fusion, f32[2048]{0:T(1024)S(1)} %broadcast.95, f32[]{:T(128)} %constant.76.clone.1), kind=kCustom, calls=%fused_computation.59 | custom fusion | flops 2048 | bytes 264 | tf_op jit(solution)/shard_map/scatter-add | solution.py:31
  53.5 126.3 %reduce-scatter.4.cloned.1.call-done = f32[64,128]{1,0:T(8,128)} async-done(((f32[4096,128]{1,0:T(8,128)}), f32[64,128]{1,0:T(8,128)}) %reduce-scatter.4.cloned.1.call-update) | async-done | bytes 32784
  179.7 0.8 copy.15
  180.6 0.9 fusion.46
  181.6 240.4 %all-reduce.5.cloned.1.call-done = f32[128,128]{0,1:T(8,128)} async-done(((f32[128,128]{0,1:T(8,128)}), f32[128,128]{0,1:T(8,128)}) %all-reduce.5.cloned.1.call-update) | async-done | bytes 65552 | tf_op jit(solution)/shard_map/psum | solution.py:63
  422.0 0.9 copy.11
  423.0 0.9 fusion.22
  423.8 11.7 %custom-call.14 = f32[128,128]{1,0:T(8,128)S(1)} custom-call(f32[128,128]{1,0:T(8,128)S(1)} %fusion.22), custom_call_target="Cholesky" | custom-call | tf_op jit(solution)/shard_map/jvp(jit(cholesky))/cholesky/custom-call.1 | solution.py:35
  435.6 0.7 compare_reduce_fusion
  436.2 0.6 fusion.24
  436.9 9.8 %custom-call.13 = f32[1,128,128]{1,2,0:T(8,128)S(1)} custom-call(f32[1,128,128]{2,1,0:T(8,128)S(1)} %fusion.24), custom_call_target="InvertDiagBlocksLowerTriangular" | custom-call | tf_op jit(solution)/shard_map/transpose(jvp(jit(cholesky)))/triangular_solve | solution.py:35
  446.7 0.2 fusion.20
  446.9 0.3 fusion.47
  447.2 1.0 fusion.29
  448.2 0.2 all-gather.2.cloned.1.call-start
  448.5 0.3 fusion.48
  448.7 233.9 %all-reduce.7.cloned.1.call-done = f32[128,128]{1,0:T(8,128)} async-done(((f32[128,128]{1,0:T(8,128)}), f32[128,128]{1,0:T(8,128)}) %all-reduce.7.cloned.1.call-update) | async-done | bytes 65552 | tf_op jit(solution)/shard_map/psum | solution.py:66
  682.6 1.1 fusion.1
  683.7 0.9 fusion
  684.6 0.2 fusion.18
  684.9 0.3 fusion.16
  685.2 0.3 fusion.12
  685.5 0.9 fusion.3
  686.4 72.9 %all-gather.2.cloned.1.call-done = bf16[4096,128]{1,0:T(8,128)(2,1)} async-done(((bf16[64,128]{1,0:T(8,128)(2,1)}), bf16[4096,128]{1,0:T(8,128)(2,1)}) %all-gather.2.cloned.1.call-update) | async-done | bytes 1048592 | tf_op jit(solution)/shard_map/all_gather | solution.py:76
  759.3 5.2 convolution_bitcast_fusion.1
  764.5 21.6 %all-reduce.9 = bf16[576,128]{0,1:T(8,128)(2,1)S(1)} all-reduce(f32[576,128]{0,1:T(8,128)} %convolution_bitcast_fusion.1), channel_id=1, replica_groups=mesh['example'=64,'feature'=4] {'feature'}, use_global_device_ids=true, to_apply=%region_7.9 | all-reduce | flops 73728 | bytes 442368 | tf_op jit(solution)/shard_map/psum | solution.py:77
  786.1 1.4 fusion.49
  787.5 3.6 add_convert_fusion
  (24 shorter events, 0.4 us)
Async XLA Ops:
  6.5 32.1 %copy-start = (s32[4096,128]{1,0:T(8,128)S(1)}, s32[4096,128]{1,0:T(8,128)}, u32[]{:S(2)}) copy-start(s32[4096,128]{1,0:T(8,128)} %param.7) | copy-start | bytes 6291460
  6.5 173.2 %reduce-scatter.4.cloned.1.call-start = ((), (), s32[]{:S(2)}) async-start(), calls=%async_computation.4 | async-start | bytes 2129920
  35.6 3.2 copy-start.3
  38.6 383.5 %all-reduce.5.cloned.1.call-start = ((), (), s32[]{:S(2)}) async-start(), calls=%async_computation.1 | async-start | bytes 131072 | tf_op jit(solution)/shard_map/psum | solution.py:63
  181.5 501.1 %all-reduce.7.cloned.1.call-start = ((), (), s32[]{:S(2)}) async-start(), calls=%async_computation.2 | async-start | bytes 131072 | tf_op jit(solution)/shard_map/psum | solution.py:66
  448.2 311.1 %all-gather.2.cloned.1.call-start = ((), (), s32[]{:S(2)}) async-start(), calls=%async_computation.3 | async-start | bytes 1064960 | tf_op jit(solution)/shard_map/all_gather | solution.py:76
  759.3 26.8 %copy-start.1 = (bf16[4096,128]{1,0:T(8,128)(2,1)S(1)}, bf16[4096,128]{1,0:T(8,128)(2,1)}, u32[]{:S(2)}) copy-start(bf16[4096,128]{1,0:T(8,128)(2,1)} %all-gather.2.cloned.1.call-done) | copy-start | bytes 3145732
  786.1 1.4 copy-start.2
Sparse Core Ops, SparseCore 0:
  38.7 140.9 reduce-scatter.3
  186.1 235.8 all-reduce.4
  448.3 234.2 all-reduce.6
  686.6 72.6 all-gather.1
where the time goes:
time: 798 us
  waiting for transfers between devices  674 us (84%)
  blocking collectives  41.8 us (5%)
  other arithmetic  38.4 us (5%)
  matrix products  25.4 us (3%)
  between operations  13.3 us (2%)
    psum x1, waiting for transfers between devices, on_device(): lax.psum(transposed(image, image, HIGH), ('example', 'feature'))  240 us
    psum x1, waiting for transfers between devices, on_device(): lax.psum(transposed(orthonormal * row_counts[:, None], orthonormal, HIGH)...  234 us
    unnamed x5, waiting for transfers between devices  126 us
    all_gather x1, waiting for transfers between devices, on_device(): grad_low = lax.all_gather(grad_low, 'example', axis=0, tiled=True)  72.9 us
    another operation x5, other arithmetic, upper_factor(): return jnp.linalg.cholesky(gram_matrix).T  22.8 us
    psum x1, blocking collectives, on_device(): lax.psum(jnp.dot(embeddings, grad_low, preferred_element_type=jnp.float32...  21.6 us
    psum x1, blocking collectives, on_device(): lax.psum(jnp.dot(embeddings, subspace, preferred_element_type=jnp.float32...  20.2 us
  transfers between devices with their start and end apart: 4, of which 4 were waited for; matrix products, arithmetic and copies ran while one was open for 2% of the time, Pallas kernels for 0%

commit v1 on v0

--- a/solution.py
+++ b/solution.py
@@ -5,6 +5,13 @@
 
 NOISE_STEP = 1.0 / 4096.0
 HIGH = lax.Precision.HIGHEST
+
+
+def exchange_gather(x, axis, dim):
+    size = lax.axis_size(axis)
+    tiles = jnp.stack([x for _ in range(size)])
+    tiles = lax.all_to_all(tiles, axis, split_axis=0, concat_axis=0)
+    return jnp.concatenate(tiles, axis=dim)
 
 
 def transposed(former, latter, precision=None):
@@ -73,7 +80,7 @@
         :, None
     ] * jnp.dot(image, gram_inverse, precision=HIGH)
     grad_low = image_grad.astype(jnp.bfloat16)
-    grad_low = lax.all_gather(grad_low, "example", axis=0, tiled=True)
+    grad_low = exchange_gather(grad_low, "example", 0)
     back_sum = lax.psum(
         jnp.dot(embeddings, grad_low, preferred_element_type=jnp.float32), "feature"
     )

time: 798 us -> 765 us (0.959)
  waiting for transfers between devices: 674 us -> 601 us
  blocking collectives: 41.8 us -> 75 us
    all_gather x1 -> x0, waiting for transfers between devices: 72.9 us -> none  [on_device(): grad_low = lax.all_gather(grad_low, 'example', axis=0, tiled=True)]
    all_to_all x0 -> x1, blocking collectives: none -> 33.8 us  [exchange_gather(): tiles = lax.all_to_all(tiles, axis, split_axis=0, concat_axis=0)]
    unnamed x5 -> x4, waiting for transfers between devices: 126 us -> 126 us
  transfers between devices with their start and end apart: 4 -> 3, of which waited for: 4 -> 3; matrix products, arithmetic and copies ran while one was open for 2% -> 2% of each run, Pallas kernels for 0% -> 0%
where the time goes in v1:
time: 765 us; the launch traced here: 764 us
  waiting for transfers between devices  601 us (79%)
  blocking collectives  75 us (10%)
  other arithmetic  38.4 us (5%)
  matrix products  31.4 us (4%)
  between operations  13.3 us (2%)
    psum x1, waiting for transfers between devices, on_device(): lax.psum(transposed(image, image, HIGH), ('example', 'feature'))  240 us
    psum x1, waiting for transfers between devices, on_device(): lax.psum(transposed(orthonormal * row_counts[:, None], orthonormal, HIGH)...  234 us
    unnamed x4, waiting for transfers between devices  126 us
    all_to_all x1, blocking collectives, exchange_gather(): tiles = lax.all_to_all(tiles, axis, split_axis=0, concat_axis=0)  33.8 us
    another operation x5, other arithmetic, upper_factor(): return jnp.linalg.cholesky(gram_matrix).T  22.8 us
    psum x1, blocking collectives, on_device(): lax.psum(jnp.dot(embeddings, grad_low, preferred_element_type=jnp.float32...  21.1 us
    psum x1, blocking collectives, on_device(): lax.psum(jnp.dot(embeddings, subspace, preferred_element_type=jnp.float32...  20.2 us
  transfers between devices with their start and end apart: 3, of which 3 were waited for; matrix products, arithmetic and copies ran while one was open for 2% of the time, Pallas kernels for 0%

profile of v1, /device:TPU:2, one launch (start us, length us, event | category | flops | bytes accessed | tf_op | source)
XLA Modules:
  0.0 764.2 jit_solution(2596139925950020157)
XLA Ops:
  6.5 4.2 fusion.45
  10.7 20.2 %all-reduce.8 = bf16[576,128]{1,0:T(8,128)(2,1)S(1)} all-reduce(f32[576,128]{1,0:T(8,128)S(1)} %fusion.45), channel_id=1, replica_groups=mesh['example'=64,'feature'=4] {'feature'}, use_global_device_ids=true, to_apply=%region_0.0 | all-reduce | flops 73728 | bytes 442368 | tf_op jit(solution)/shard_map/psum | solution.py:57
  30.9 4.7 convolution_bitcast_fusion
  35.6 2.9 copy.14
  38.8 14.7 %scatter_custom_fusion = f32[65]{0:T(128)S(1)} fusion(s32[2048]{0:T(1024)S(1)} %and_select_fusion, f32[2048]{0:T(1024)S(1)} %broadcast.97, f32[]{:T(128)} %constant.76.clone.1), kind=kCustom, calls=%fused_computation.59 | custom fusion | flops 2048 | bytes 264 | tf_op jit(solution)/shard_map/scatter-add | solution.py:38
  53.5 126.3 %reduce-scatter.4.cloned.1.call-done = f32[64,128]{1,0:T(8,128)} async-done(((f32[4096,128]{1,0:T(8,128)}), f32[64,128]{1,0:T(8,128)}) %reduce-scatter.4.cloned.1.call-update) | async-done | bytes 32784
  179.7 0.8 copy.15
  180.6 0.9 fusion.46
  181.5 0.2 all-reduce.7.cloned.1.call-start
  181.8 240.3 %all-reduce.5.cloned.1.call-done = f32[128,128]{0,1:T(8,128)} async-done(((f32[128,128]{0,1:T(8,128)}), f32[128,128]{0,1:T(8,128)}) %all-reduce.5.cloned.1.call-update) | async-done | bytes 65552 | tf_op jit(solution)/shard_map/psum | solution.py:70
  422.0 0.9 copy.11
  423.0 0.9 fusion.22
  423.8 11.7 %custom-call.14 = f32[128,128]{1,0:T(8,128)S(1)} custom-call(f32[128,128]{1,0:T(8,128)S(1)} %fusion.22), custom_call_target="Cholesky" | custom-call | tf_op jit(solution)/shard_map/jvp(jit(cholesky))/cholesky/custom-call.1 | solution.py:42
  435.6 0.7 compare_reduce_fusion
  436.2 0.6 fusion.24
  436.9 9.8 %custom-call.13 = f32[1,128,128]{1,2,0:T(8,128)S(1)} custom-call(f32[1,128,128]{2,1,0:T(8,128)S(1)} %fusion.24), custom_call_target="InvertDiagBlocksLowerTriangular" | custom-call | tf_op jit(solution)/shard_map/transpose(jvp(jit(cholesky)))/triangular_solve | solution.py:42
  446.7 0.2 fusion.20
  446.9 0.3 fusion.47
  447.2 1.0 fusion.29
  448.2 0.3 fusion.48
  448.5 234.1 %all-reduce.7.cloned.1.call-done = f32[128,128]{1,0:T(8,128)} async-done(((f32[128,128]{1,0:T(8,128)}), f32[128,128]{1,0:T(8,128)}) %all-reduce.7.cloned.1.call-update) | async-done | bytes 65552 | tf_op jit(solution)/shard_map/psum | solution.py:73
  682.6 1.1 fusion.1
  683.7 0.9 fusion
  684.9 0.3 fusion.16
  685.2 0.3 fusion.12
  685.5 0.3 fusion.3
  685.8 0.2 stack.2
  686.1 33.8 %all_to_all.5 = bf16[64,64,128]{2,1,0:T(8,128)(2,1)S(1)} all-to-all(bf16[64,64,128]{2,1,0:T(8,128)(2,1)S(1)} %stack.2), channel_id=1, replica_groups=mesh['example'=64,'feature'=4] {'example'}, dimensions={0} | all-to-all | bytes 2097152 | tf_op jit(solution)/shard_map/all_to_all | solution.py:13
  719.8 4.1 convolution_bitcast_fusion.1
  724.0 5.0 fusion.49
  729.0 21.1 %all-reduce.9 = bf16[576,128]{0,1:T(8,128)(2,1)S(1)} all-reduce(f32[576,128]{0,1:T(8,128)S(1)} %convolution_bitcast_fusion.1), channel_id=1, replica_groups=mesh['example'=64,'feature'=4] {'feature'}, use_global_device_ids=true, to_apply=%region_7.9 | all-reduce | flops 73728 | bytes 442368 | tf_op jit(solution)/shard_map/psum | solution.py:84
  750.1 7.6 add_convert_fusion
  (19 shorter events, 0.6 us)
Async XLA Ops:
  6.5 32.1 %copy-start = (s32[4096,128]{1,0:T(8,128)S(1)}, s32[4096,128]{1,0:T(8,128)}, u32[]{:S(2)}) copy-start(s32[4096,128]{1,0:T(8,128)} %param.7) | copy-start | bytes 6291460
  6.5 173.2 %reduce-scatter.4.cloned.1.call-start = ((), (), s32[]{:S(2)}) async-start(), calls=%async_computation.4 | async-start | bytes 2129920
  35.6 3.2 copy-start.1
  38.6 383.5 %all-reduce.5.cloned.1.call-start = ((), (), s32[]{:S(2)}) async-start(), calls=%async_computation.2 | async-start | bytes 131072 | tf_op jit(solution)/shard_map/psum | solution.py:70
  181.5 501.1 %all-reduce.7.cloned.1.call-start = ((), (), s32[]{:S(2)}) async-start(), calls=%async_computation.3 | async-start | bytes 131072 | tf_op jit(solution)/shard_map/psum | solution.py:73
Sparse Core Ops, SparseCore 0:
  38.7 140.9 reduce-scatter.3
  186.1 235.8 all-reduce.4
  448.3 234.2 all-reduce.6

commit v2 on v0

--- a/solution.py
+++ b/solution.py
@@ -5,6 +5,12 @@
 
 NOISE_STEP = 1.0 / 4096.0
 HIGH = lax.Precision.HIGHEST
+
+
+def push_sections(q_in, mesh_name, row_axis):
+    for pp in (mesh_name, row_axis):
+        q_in = lax.psum(q_in, pp)
+    return q_in
 
 
 def transposed(former, latter, precision=None):
@@ -63,8 +69,8 @@
     gram_matrix = lax.psum(transposed(image, image, HIGH), ("example", "feature"))
     inverse_factor, gram_inverse = factorize(gram_matrix)
     orthonormal = jnp.dot(image, inverse_factor.T, precision=HIGH)
-    alignment = lax.psum(
-        transposed(orthonormal * row_counts[:, None], orthonormal, HIGH), ("example", "feature")
+    alignment = push_sections(
+        transposed(orthonormal * row_counts[:, None], orthonormal, HIGH), "feature", "example"
     )
     factor_grad = 2.0 * jnp.dot(alignment, inverse_factor, precision=HIGH)
     unused, pull_back = jax.vjp(upper_factor, gram_matrix)

time: 798 us -> 778 us (0.975)
  waiting for transfers between devices: 674 us -> 654 us
    psum x1 -> x2, waiting for transfers between devices: 234 us -> 214 us  [push_sections(): q_in = lax.psum(q_in, pp)]
    unnamed x5 -> x6, waiting for transfers between devices: 126 us -> 126 us
  transfers between devices with their start and end apart: 4 -> 5, of which waited for: 4 -> 5; matrix products, arithmetic and copies ran while one was open for 2% -> 2% of each run, Pallas kernels for 0% -> 0%
where the time goes in v2:
time: 778 us
  waiting for transfers between devices  654 us (84%)
  blocking collectives  41.8 us (5%)
  other arithmetic  38.3 us (5%)
  matrix products  25.4 us (3%)
  between operations  13.4 us (2%)
    psum x1, waiting for transfers between devices, on_device(): lax.psum(transposed(image, image, HIGH), ('example', 'feature'))  240 us
    psum x2, waiting for transfers between devices, push_sections(): q_in = lax.psum(q_in, pp)  214 us
    unnamed x6, waiting for transfers between devices  126 us
    all_gather x1, waiting for transfers between devices, on_device(): grad_low = lax.all_gather(grad_low, 'example', axis=0, tiled=True)  73.3 us
    another operation x5, other arithmetic, upper_factor(): return jnp.linalg.cholesky(gram_matrix).T  22.8 us
    psum x1, blocking collectives, on_device(): lax.psum(jnp.dot(embeddings, grad_low, preferred_element_type=jnp.float32...  21.6 us
    psum x1, blocking collectives, on_device(): lax.psum(jnp.dot(embeddings, subspace, preferred_element_type=jnp.float32...  20.2 us
  transfers between devices with their start and end apart: 5, of which 5 were waited for; matrix products, arithmetic and copies ran while one was open for 2% of the time, Pallas kernels for 0%

profile of v2, /device:TPU:2, one launch (start us, length us, event | category | flops | bytes accessed | tf_op | source)
XLA Modules:
  0.0 778.0 jit_solution(15669929040957145166)
XLA Ops:
  6.5 4.2 fusion.45
  10.7 20.2 %all-reduce.11 = bf16[576,128]{1,0:T(8,128)(2,1)S(1)} all-reduce(f32[576,128]{1,0:T(8,128)S(1)} %fusion.45), channel_id=1, replica_groups=mesh['example'=64,'feature'=4] {'feature'}, use_global_device_ids=true, to_apply=%region_0.0 | all-reduce | flops 73728 | bytes 442368 | tf_op jit(solution)/shard_map/psum | solution.py:56
  30.9 4.7 convolution_bitcast_fusion
  35.6 2.9 copy.14
  38.8 14.7 %scatter_custom_fusion = f32[65]{0:T(128)S(1)} fusion(s32[2048]{0:T(1024)S(1)} %and_select_fusion, f32[2048]{0:T(1024)S(1)} %broadcast.95, f32[]{:T(128)} %constant.76.clone.1), kind=kCustom, calls=%fused_computation.59 | custom fusion | flops 2048 | bytes 264 | tf_op jit(solution)/shard_map/scatter-add | solution.py:37
  53.4 126.3 %reduce-scatter.4.cloned.1.call-done = f32[64,128]{1,0:T(8,128)} async-done(((f32[4096,128]{1,0:T(8,128)}), f32[64,128]{1,0:T(8,128)}) %reduce-scatter.4.cloned.1.call-update) | async-done | bytes 32784
  179.7 0.8 copy.15
  180.6 0.9 fusion.46
  181.6 240.4 %all-reduce.6.cloned.1.call-done = f32[128,128]{0,1:T(8,128)} async-done(((f32[128,128]{0,1:T(8,128)}), f32[128,128]{0,1:T(8,128)}) %all-reduce.6.cloned.1.call-update) | async-done | bytes 65552 | tf_op jit(solution)/shard_map/psum | solution.py:69
  422.0 0.9 copy.11
  423.0 0.9 fusion.22
  423.8 11.7 %custom-call.14 = f32[128,128]{1,0:T(8,128)S(1)} custom-call(f32[128,128]{1,0:T(8,128)S(1)} %fusion.22), custom_call_target="Cholesky" | custom-call | tf_op jit(solution)/shard_map/jvp(jit(cholesky))/cholesky/custom-call.1 | solution.py:41
  435.6 0.6 compare_reduce_fusion
  436.2 0.6 fusion.24
  436.8 9.8 %custom-call.13 = f32[1,128,128]{1,2,0:T(8,128)S(1)} custom-call(f32[1,128,128]{2,1,0:T(8,128)S(1)} %fusion.24), custom_call_target="InvertDiagBlocksLowerTriangular" | custom-call | tf_op jit(solution)/shard_map/transpose(jvp(jit(cholesky)))/triangular_solve | solution.py:41
  446.6 0.2 fusion.20
  446.8 0.3 fusion.47
  447.1 1.0 fusion.29
  448.2 43.3 %all-reduce.8.cloned.1.call-done = f32[128,128]{1,0:T(8,128)} async-done(((f32[128,128]{1,0:T(8,128)}), f32[128,128]{1,0:T(8,128)}) %all-reduce.8.cloned.1.call-update) | async-done | bytes 65552 | tf_op jit(solution)/shard_map/psum | solution.py:12
  491.5 0.2 all-gather.2.cloned.1.call-start
  491.7 0.3 fusion.48
  492.0 170.6 %all-reduce.10.cloned.1.call-done = f32[128,128]{1,0:T(8,128)} async-done(((f32[128,128]{1,0:T(8,128)}), f32[128,128]{1,0:T(8,128)}) %all-reduce.10.cloned.1.call-update) | async-done | bytes 65552 | tf_op jit(solution)/shard_map/psum | solution.py:12
  662.6 1.1 fusion.1
  663.7 0.8 fusion
  664.8 0.3 fusion.16
  665.2 0.3 fusion.12
  665.5 0.9 fusion.3
  666.4 73.3 %all-gather.2.cloned.1.call-done = bf16[4096,128]{1,0:T(8,128)(2,1)} async-done(((bf16[64,128]{1,0:T(8,128)(2,1)}), bf16[4096,128]{1,0:T(8,128)(2,1)}) %all-gather.2.cloned.1.call-update) | async-done | bytes 1048592 | tf_op jit(solution)/shard_map/all_gather | solution.py:82
  739.7 5.2 convolution_bitcast_fusion.1
  744.9 21.6 %all-reduce.12 = bf16[576,128]{0,1:T(8,128)(2,1)S(1)} all-reduce(f32[576,128]{0,1:T(8,128)} %convolution_bitcast_fusion.1), channel_id=1, replica_groups=mesh['example'=64,'feature'=4] {'feature'}, use_global_device_ids=true, to_apply=%region_8.10 | all-reduce | flops 73728 | bytes 442368 | tf_op jit(solution)/shard_map/psum | solution.py:83
  766.5 1.4 fusion.49
  767.9 3.6 add_convert_fusion
  (27 shorter events, 0.7 us)
Async XLA Ops:
  6.5 32.1 %copy-start = (s32[4096,128]{1,0:T(8,128)S(1)}, s32[4096,128]{1,0:T(8,128)}, u32[]{:S(2)}) copy-start(s32[4096,128]{1,0:T(8,128)} %param.7) | copy-start | bytes 6291460
  6.5 173.2 %reduce-scatter.4.cloned.1.call-start = ((), (), s32[]{:S(2)}) async-start(), calls=%async_computation.5 | async-start | bytes 2129920
  35.6 3.2 copy-start.3
  38.6 383.5 %all-reduce.6.cloned.1.call-start = ((), (), s32[]{:S(2)}) async-start(), calls=%async_computation.1 | async-start | bytes 131072 | tf_op jit(solution)/shard_map/psum | solution.py:69
  181.5 309.9 %all-reduce.8.cloned.1.call-start = ((), (), s32[]{:S(2)}) async-start(), calls=%async_computation.2 | async-start | bytes 131072 | tf_op jit(solution)/shard_map/psum | solution.py:12
  448.1 214.5 %all-reduce.10.cloned.1.call-start = ((), (), s32[]{:S(2)}) async-start(), calls=%async_computation.3 | async-start | bytes 131072 | tf_op jit(solution)/shard_map/psum | solution.py:12
  491.5 248.2 %all-gather.2.cloned.1.call-start = ((), (), s32[]{:S(2)}) async-start(), calls=%async_computation.4 | async-start | bytes 1064960 | tf_op jit(solution)/shard_map/all_gather | solution.py:82
  739.7 26.8 %copy-start.1 = (bf16[4096,128]{1,0:T(8,128)(2,1)S(1)}, bf16[4096,128]{1,0:T(8,128)(2,1)}, u32[]{:S(2)}) copy-start(bf16[4096,128]{1,0:T(8,128)(2,1)} %all-gather.2.cloned.1.call-done) | copy-start | bytes 3145732
  766.5 1.4 copy-start.2
Sparse Core Ops, SparseCore 0:
  38.7 140.9 reduce-scatter.3
  186.1 235.8 all-reduce.5
  448.3 43.1 all-reduce.7
  494.8 167.7 all-reduce.9
  666.5 73.1 all-gather.1
